TPU v7x, 32 devices: a whole 2x2x4 slice. The times are simulated.
32 devices in a mesh: row: 4 (over x, core), col: 8 (over z, y).
Axes of the slice: x: 2, y: 2, z: 4, core: 2. Of those that a mesh axis runs over, the one named last changes fastest.
Arguments:
- t_slab: bfloat16 [4, 2, 512, 64], P('row', None, 'col'), may hold values from -6 to 6
- w_cycle: bfloat16 [128, 16384], P('row', 'col'), may hold values from -0.5 to 0.5
Outputs:
- t_amp: bfloat16 [2048, 128], P('row', 'col')
- cycle_z: float32 [2048, 16384], P('row', 'col')
All inputs are finite; a program needn't handle non-finite values.
Results may differ from a plain program's by a relative error of at most 0.001.
Values may be sent and summed in bfloat16 or wider, within the bound.
A program may use at most 64 MiB of HBM per device.

v0:
```python
import jax
import jax.numpy as jnp
from jax import lax
from jax.sharding import PartitionSpec as P


def shards(t_slab, w_cycle):
    local_rows = jnp.transpose(t_slab[0], (1, 0, 2)).reshape(
        t_slab.shape[2], t_slab.shape[1] * t_slab.shape[3]
    )
    t_tile = lax.all_to_all(local_rows, "col", split_axis=1, concat_axis=0, tiled=True)
    t_full = lax.all_gather(t_tile, "col", axis=1, tiled=True)
    w_full = lax.all_gather(w_cycle, "row", axis=0, tiled=True)
    cycle_z = jnp.dot(t_full, w_full, preferred_element_type=jnp.float32)
    return (t_tile, cycle_z)


def solution(mesh):
    placed = (P("row", None, "col", None), P("row", "col"))
    return jax.shard_map(
        shards,
        mesh=mesh,
        in_specs=placed,
        out_specs=(P("row", "col"), P("row", "col")),
        check_vma=False,
    )
```

profile of v0, /device:TPU:0, one launch (start us, length us, event | category | flops | bytes accessed | tf_op | source)
XLA Modules:
  0.0 50.9 jit_solution(17427372366816520272)
XLA Ops:
  0.6 0.8 %copy.5 = bf16[1,2,64,64]{2,3,1,0:T(8,128)(2,1)S(1)} copy(bf16[1,2,64,64]{3,2,1,0:T(8,128)(2,1)} %param.2) | data formatting | bytes 32768 | tf_op args[0]
  1.5 0.7 %reshape.9 = bf16[8,2,512]{2,1,0:T(2,128)(2,1)} reshape(bf16[8,16,64]{2,1,0:T(8,128)(2,1)S(1)} %bitcast.14) | data formatting | bytes 32768
  2.2 7.3 %all-to-all-start = ((bf16[8,2,512]{2,1,0:T(2,128)(2,1)}), bf16[8,2,512]{2,1,0:T(2,128)(2,1)S(1)}, u32[]{:S(2)}, u32[]{:S(2)}) async-start(bf16[8,2,512]{2,1,0:T(2,128)(2,1)} %reshape.9), calls=%async_computation | async-start | bytes 32768 | tf_op jit(solution)/shard_map/all_to_all | solution.py:11
  9.5 7.4 %all_gather.7 = bf16[128,2048]{1,0:T(8,128)(2,1)S(1)} all-gather(bf16[32,2048]{1,0:T(8,128)(2,1)} %param.3), channel_id=1, replica_groups=mesh['row'=4,'col'=8] {'row'}, dimensions={0}, use_global_device_ids=true | all-gather | bytes 655360 | tf_op jit(solution)/shard_map/all_gather | solution.py:13
  16.8 0.0 all-to-all-done
  16.8 0.1 reshape.10
  17.0 0.1 all_to_all.17
  17.1 0.0 copy-start
  17.1 31.1 %all_gather.6 = bf16[512,128]{0,1:T(8,128)(2,1)S(1)} all-gather(bf16[512,16]{0,1:T(8,128)(2,1)S(1)} %all_to_all.17), channel_id=1, replica_groups=mesh['row'=4,'col'=8] {'col'}, dimensions={1}, use_global_device_ids=true | all-gather | bytes 147456 | tf_op jit(solution)/shard_map/all_gather | solution.py:12
  48.2 2.7 %fusion = f32[512,2048]{1,0:T(8,128)} fusion(bf16[512,128]{0,1:T(8,128)(2,1)S(1)} %all_gather.6, bf16[128,2048]{1,0:T(8,128)(2,1)S(1)} %all_gather.7), kind=kOutput, calls=%fused_computation.1 | convolution fusion | flops 268435456 | bytes 4849664 | tf_op jit(solution)/shard_map/dot_general | solution.py:14
  50.9 0.0 copy-done
  (2 shorter events, 0.0 us)
Async XLA Ops:
  2.2 14.7 %all-to-all-start = ((bf16[8,2,512]{2,1,0:T(2,128)(2,1)}), bf16[8,2,512]{2,1,0:T(2,128)(2,1)S(1)}, u32[]{:S(2)}, u32[]{:S(2)}) async-start(bf16[8,2,512]{2,1,0:T(2,128)(2,1)} %reshape.9), calls=%async_computation | async-start | bytes 32768 | tf_op jit(solution)/shard_map/all_to_all | solution.py:11
  17.1 33.8 %copy-start = (bf16[512,16]{0,1:T(8,128)(2,1)}, bf16[512,16]{0,1:T(8,128)(2,1)S(1)}, u32[]{:S(2)}) copy-start(bf16[512,16]{0,1:T(8,128)(2,1)S(1)} %all_to_all.17) | copy-start | bytes 49156
where the time goes:
time: 51.2 us; the launch traced here: 50.9 us
  blocking collectives  38.4 us (75%)
  starting transfers between devices  7.28 us (14%)
  matrix products  2.74 us (5%)
  local copies, waits for them, and re-layouts  1.77 us (3%)
  between operations  0.66 us (1%)
    all_gather x1, blocking collectives, shards(): t_full = lax.all_gather(t_tile, 'col', axis=1, tiled=True)  31.1 us
    all_gather x1, blocking collectives, shards(): w_full = lax.all_gather(w_cycle, 'row', axis=0, tiled=True)  7.37 us
    all_to_all x1, starting transfers between devices, shards(): lax.all_to_all(local_rows, 'col', split_axis=1, concat_axis=0, tiled=True)  7.28 us
    dot_general x1, matrix products, shards(): cycle_z = jnp.dot(t_full, w_full, preferred_element_type=jnp.float32)  2.74 us
    unnamed x5, local copies, waits for them, and re-layouts  1.65 us
  transfers between devices with their start and end apart: 1, of which 0 were waited for; matrix products, arithmetic and copies ran while one was open for 0% of the time, Pallas kernels for 0%

commit v1 on v0

--- a/solution.py
+++ b/solution.py
@@ -9,7 +9,15 @@
         t_slab.shape[2], t_slab.shape[1] * t_slab.shape[3]
     )
     t_tile = lax.all_to_all(local_rows, "col", split_axis=1, concat_axis=0, tiled=True)
-    t_full = lax.all_gather(t_tile, "col", axis=1, tiled=True)
+    ways, here = (lax.axis_size("col"), lax.axis_index("col"))
+    grown, reach = (t_tile, 1)
+    while reach < ways:
+        theirs = lax.ppermute(grown, "col", [(d, d ^ reach) for d in range(ways)])
+        mine_first = jnp.concatenate([grown, theirs], axis=1)
+        theirs_first = jnp.concatenate([theirs, grown], axis=1)
+        grown = jnp.where(here & reach == 0, mine_first, theirs_first)
+        reach = 2 * reach
+    t_full = grown
     w_full = lax.all_gather(w_cycle, "row", axis=0, tiled=True)
     cycle_z = jnp.dot(t_full, w_full, preferred_element_type=jnp.float32)
     return (t_tile, cycle_z)

time: 51.2 us -> 34.6 us (0.68)
  blocking collectives: 38.4 us -> 21 us
  waiting for transfers between devices: 0.01 us -> 6.95 us
  starting transfers between devices: 7.28 us -> 1.79 us
  local copies, waits for them, and re-layouts: 1.77 us -> 1.16 us
    all_gather x1 -> x0, blocking collectives: 31.1 us -> none  [shards(): t_full = lax.all_gather(t_tile, 'col', axis=1, tiled=True)]
    all_to_all x0 -> x1, blocking collectives: none -> 13.7 us  [shards(): lax.all_to_all(local_rows, 'col', split_axis=1, concat_axis=0, tiled=True)]
    all_to_all x1 -> x0, starting transfers between devices: 7.28 us -> none  [shards(): lax.all_to_all(local_rows, 'col', split_axis=1, concat_axis=0, tiled=True)]
    ppermute x0 -> x3, waiting for transfers between devices: none -> 6.95 us  [shards(): theirs = lax.ppermute(grown, 'col', [(d, d ^ reach) for d in range(ways)])]
    ppermute x0 -> x3, starting transfers between devices: none -> 1.79 us  [shards(): theirs = lax.ppermute(grown, 'col', [(d, d ^ reach) for d in range(ways)])]
    unnamed x5, local copies, waits for them, and re-layouts: 1.65 us -> 1.04 us
  transfers between devices with their start and end apart: 1 -> 3, of which waited for: 0 -> 2; matrix products, arithmetic and copies ran while one was open for 0% -> 0% of each run, Pallas kernels for 0% -> 0%
where the time goes in v1:
time: 34.6 us; the launch traced here: 34.4 us
  blocking collectives  21 us (61%)
  waiting for transfers between devices  6.95 us (20%)
  matrix products  2.75 us (8%)
  starting transfers between devices  1.79 us (5%)
  local copies, waits for them, and re-layouts  1.16 us (3%)
  between operations  0.67 us (2%)
    all_to_all x1, blocking collectives, shards(): lax.all_to_all(local_rows, 'col', split_axis=1, concat_axis=0, tiled=True)  13.7 us
    all_gather x1, blocking collectives, shards(): w_full = lax.all_gather(w_cycle, 'row', axis=0, tiled=True)  7.37 us
    ppermute x3, waiting for transfers between devices, shards(): theirs = lax.ppermute(grown, 'col', [(d, d ^ reach) for d in range(ways)])  6.95 us
    dot_general x1, matrix products, shards(): cycle_z = jnp.dot(t_full, w_full, preferred_element_type=jnp.float32)  2.75 us
    ppermute x3, starting transfers between devices, shards(): theirs = lax.ppermute(grown, 'col', [(d, d ^ reach) for d in range(ways)])  1.79 us
    unnamed x5, local copies, waits for them, and re-layouts  1.04 us
  transfers between devices with their start and end apart: 3, of which 2 were waited for; matrix products, arithmetic and copies ran while one was open for 0% of the time, Pallas kernels for 0%

profile of v1, /device:TPU:0, one launch (start us, length us, event | category | flops | bytes accessed | tf_op | source)
XLA Modules:
  0.0 34.4 jit_solution(5344128521617647981)
XLA Ops:
  0.6 0.8 %copy.5 = bf16[1,2,64,64]{2,3,1,0:T(8,128)(2,1)S(1)} copy(bf16[1,2,64,64]{3,2,1,0:T(8,128)(2,1)} %param.2) | data formatting | bytes 32768 | tf_op args[0]
  1.5 0.1 reshape.9
  1.6 13.7 %all_to_all.19 = bf16[8,2,512]{2,1,0:T(2,128)(2,1)S(1)} all-to-all(bf16[8,2,512]{2,1,0:T(2,128)(2,1)S(1)} %reshape.9), channel_id=1, replica_groups=mesh['row'=4,'col'=8] {'col'}, dimensions={0} | all-to-all | bytes 32768 | tf_op jit(solution)/shard_map/all_to_all | solution.py:11
  15.2 0.1 reshape.10
  15.4 0.1 all_to_all.17
  15.5 0.0 copy-start
  15.5 0.6 %collective-permute-start = (bf16[512,16]{0,1:T(8,128)(2,1)S(1)}, bf16[512,16]{0,1:T(8,128)(2,1)S(1)}, u32[]{:S(2)}, u32[]{:S(2)}) collective-permute-start(bf16[512,16]{0,1:T(8,128)(2,1)S(1)} %all_to_all.17), channel_id=1, source_target_pairs={{0,1},{1,0},{2,3},{3,2},{4,5},{5,4},{6,7},{7,6},{8,9},{9,8},{10,11... | collective-permute-start | bytes 49160 | tf_op jit(solution)/shard_map/ppermute | solution.py:15
  16.1 3.2 %collective-permute-done = bf16[512,16]{0,1:T(8,128)(2,1)S(1)} collective-permute-done((bf16[512,16]{0,1:T(8,128)(2,1)S(1)}, bf16[512,16]{0,1:T(8,128)(2,1)S(1)}, u32[]{:S(2)}, u32[]{:S(2)}) %collective-permute-start) | collective-permute-done | bytes 16416 | tf_op jit(solution)/shard_map/ppermute | solution.py:15
  19.3 0.5 %collective-permute-start.1 = (bf16[512,32]{0,1:T(8,128)(2,1)S(1)}, bf16[512,32]{0,1:T(8,128)(2,1)S(1)}, u32[]{:S(2)}, u32[]{:S(2)}) collective-permute-start(bf16[512,32]{0,1:T(8,128)(2,1)S(1)} %maximum_select_fusion.3), channel_id=1, source_target_pairs={{0,2},{1,3},{2,0},{3,1},{4,6},{5,7},{6,4},{7,5},{8,10},{9,11},{10,... | collective-permute-start | bytes 98312 | tf_op jit(solution)/shard_map/ppermute | solution.py:15
  19.8 3.7 %collective-permute-done.1 = bf16[512,32]{0,1:T(8,128)(2,1)S(1)} collective-permute-done((bf16[512,32]{0,1:T(8,128)(2,1)S(1)}, bf16[512,32]{0,1:T(8,128)(2,1)S(1)}, u32[]{:S(2)}, u32[]{:S(2)}) %collective-permute-start.1) | collective-permute-done | bytes 32800 | tf_op jit(solution)/shard_map/ppermute | solution.py:15
  23.6 0.7 %collective-permute-start.2 = (bf16[512,64]{0,1:T(8,128)(2,1)S(1)}, bf16[512,64]{0,1:T(8,128)(2,1)S(1)}, u32[]{:S(2)}, u32[]{:S(2)}) collective-permute-start(bf16[512,64]{0,1:T(8,128)(2,1)S(1)} %maximum_select_fusion.2), channel_id=1, source_target_pairs={{0,4},{1,5},{2,6},{3,7},{4,0},{5,1},{6,2},{7,3},{8,12},{9,13},{10,... | collective-permute-start | bytes 196616 | tf_op jit(solution)/shard_map/ppermute | solution.py:15
  24.2 7.4 %all_gather.3 = bf16[128,2048]{1,0:T(8,128)(2,1)S(1)} all-gather(bf16[32,2048]{1,0:T(8,128)(2,1)} %param.3), channel_id=1, replica_groups=mesh['row'=4,'col'=8] {'row'}, dimensions={0}, use_global_device_ids=true | all-gather | bytes 655360 | tf_op jit(solution)/shard_map/all_gather | solution.py:21
  31.6 0.0 collective-permute-done.2
  31.6 2.7 %fusion = f32[512,2048]{1,0:T(8,128)} fusion(bf16[128,2048]{1,0:T(8,128)(2,1)S(1)} %all_gather.3, bf16[512,64]{0,1:T(8,128)(2,1)S(1)} %collective-permute-done.2, bf16[512,64]{0,1:T(8,128)(2,1)S(1)} %maximum_select_fusion.2, pred[]{:T(512)S(6)} %eq.9), kind=kOutput, calls=%fused_computation.1 | convolution fusion | flops 269025280 | bytes 4849665 | tf_op jit(solution)/shard_map/dot_general | solution.py:22
  34.4 0.0 copy-done
  (4 shorter events, 0.0 us)
Async XLA Ops:
  15.5 18.9 %copy-start = (bf16[512,16]{0,1:T(8,128)(2,1)}, bf16[512,16]{0,1:T(8,128)(2,1)S(1)}, u32[]{:S(2)}) copy-start(bf16[512,16]{0,1:T(8,128)(2,1)S(1)} %all_to_all.17) | copy-start | bytes 49156
  15.5 3.8 %collective-permute-start = (bf16[512,16]{0,1:T(8,128)(2,1)S(1)}, bf16[512,16]{0,1:T(8,128)(2,1)S(1)}, u32[]{:S(2)}, u32[]{:S(2)}) collective-permute-start(bf16[512,16]{0,1:T(8,128)(2,1)S(1)} %all_to_all.17), channel_id=1, source_target_pairs={{0,1},{1,0},{2,3},{3,2},{4,5},{5,4},{6,7},{7,6},{8,9},{9,8},{10,11... | collective-permute-start | bytes 49160 | tf_op jit(solution)/shard_map/ppermute | solution.py:15
  19.3 4.3 %collective-permute-start.1 = (bf16[512,32]{0,1:T(8,128)(2,1)S(1)}, bf16[512,32]{0,1:T(8,128)(2,1)S(1)}, u32[]{:S(2)}, u32[]{:S(2)}) collective-permute-start(bf16[512,32]{0,1:T(8,128)(2,1)S(1)} %maximum_select_fusion.3), channel_id=1, source_target_pairs={{0,2},{1,3},{2,0},{3,1},{4,6},{5,7},{6,4},{7,5},{8,10},{9,11},{10,... | collective-permute-start | bytes 98312 | tf_op jit(solution)/shard_map/ppermute | solution.py:15
  23.6 8.0 %collective-permute-start.2 = (bf16[512,64]{0,1:T(8,128)(2,1)S(1)}, bf16[512,64]{0,1:T(8,128)(2,1)S(1)}, u32[]{:S(2)}, u32[]{:S(2)}) collective-permute-start(bf16[512,64]{0,1:T(8,128)(2,1)S(1)} %maximum_select_fusion.2), channel_id=1, source_target_pairs={{0,4},{1,5},{2,6},{3,7},{4,0},{5,1},{6,2},{7,3},{8,12},{9,13},{10,... | collective-permute-start | bytes 196616 | tf_op jit(solution)/shard_map/ppermute | solution.py:15
